TPU v7x, 32 devices: a whole 2x2x4 slice. The times are simulated.
32 devices in a mesh: grid: 2 (over y), member: 8 (over z, x), sample: 2 (over core).
Axes of the slice: x: 2, y: 2, z: 4, core: 2. Of those that a mesh axis runs over, the one named last changes fastest.
Arguments:
- hidden_states: bfloat16 [2, 8, 2048, 1024], P('sample', 'member', 'grid'), may hold values from -6 to 6
- targets: float32 [2, 100, 2048], P('sample', None, 'grid'), may hold values from -6 to 6
- area_weight: float32 [2048], P('grid'), may hold values from 0.2 to 2
- var_weight: float32 [100], replicated, may hold values from 0.25 to 4
- weight_in: bfloat16 [1024, 1024], replicated, may hold values from -0.1875 to 0.1875
- bias_in: float32 [1024], replicated, may hold values from -3 to 3
- output_weight: bfloat16 [1024, 100], replicated, may hold values from -0.1875 to 0.1875
- output_bias: float32 [100], replicated, may hold values from -3 to 3
Outputs:
- grad_weight_in: float32 [1024, 1024], P(('grid', 'member'))
- grad_bias_in: float32 [1024], P(('grid', 'member'))
- grad_weight_out: float32 [1024, 100], P(('grid', 'member'))
All inputs are finite; a program needn't handle non-finite values.
Results may differ from a plain program's by a relative error of at most 0.0058.
Values may be sent and summed in bfloat16 or wider, within the bound.
A program may use at most 64 MiB of HBM per device.

v0:
```python
import math

import jax
import jax.numpy as jnp
from jax import lax
from jax.sharding import PartitionSpec as P

smoothing = 0.01
alpha_fair = 0.95


def softened_slope(value):
    return value * lax.rsqrt(value * value + smoothing)


def local(
    hidden_states, targets, area_weight, var_weight, weight_in, bias_in, output_weight, output_bias
):
    inputs = hidden_states[0, 0]
    num_points = inputs.shape[0]
    member_stack = lax.axis_size("member")
    samples = lax.axis_size("sample")
    all_points = lax.axis_size("grid") * num_points
    pre_activation = jnp.dot(inputs, weight_in, preferred_element_type=jnp.float32) + bias_in
    hidden_activation = jax.nn.gelu(pre_activation).astype(jnp.bfloat16)
    member_prediction = (
        lax.dot_general(
            output_weight,
            hidden_activation,
            (((0,), (1,)), ((), ())),
            preferred_element_type=jnp.float32,
        )
        + output_bias[:, None]
    )
    eps_fair = (1.0 - alpha_fair) / member_stack
    pairwise_coefficient = (1.0 - eps_fair) / (member_stack * (member_stack - 1))
    loss_scale = member_stack / math.sqrt(samples * all_points)
    latitude_weighting = loss_scale * area_weight[None, :] * var_weight[:, None]
    observed_rows = targets[0]
    pairwise_total = jnp.sum(
        softened_slope(
            member_prediction[None]
            - lax.all_gather(member_prediction[None], "member", axis=0, tiled=True)
        ),
        axis=0,
    )
    prediction_gradient = latitude_weighting * (
        softened_slope(member_prediction - observed_rows) / member_stack
        - pairwise_coefficient * pairwise_total
    )
    gradient_rows = prediction_gradient.astype(jnp.bfloat16)
    act_grad = lax.dot_general(
        gradient_rows, output_weight, (((0,), (1,)), ((), ())), preferred_element_type=jnp.float32
    )
    unused_value, gelu_back = jax.vjp(jax.nn.gelu, pre_activation)
    preact_grad_f = gelu_back(act_grad)[0]
    preact_grad = preact_grad_f.astype(jnp.bfloat16)
    grad_in = lax.dot_general(
        inputs, preact_grad, (((0,), (0,)), ((), ())), preferred_element_type=jnp.float32
    )
    grad_bias = jnp.sum(preact_grad_f, axis=0)
    grad_out = lax.dot_general(
        hidden_activation,
        gradient_rows,
        (((0,), (1,)), ((), ())),
        preferred_element_type=jnp.float32,
    )
    shares = (
        lax.psum_scatter(grad_in, ("grid", "member"), scatter_dimension=0, tiled=True),
        lax.psum_scatter(grad_bias, ("grid", "member"), scatter_dimension=0, tiled=True),
        lax.psum_scatter(grad_out, ("grid", "member"), scatter_dimension=0, tiled=True),
    )
    totals = lax.psum((shares[0], shares[1], shares[2]), "sample")
    return (totals[0], totals[1], totals[2])


def solution(mesh):
    placed = (
        P("sample", "member", "grid", None),
        P("sample", None, "grid"),
        P("grid"),
        P(),
        P(),
        P(),
        P(),
        P(),
    )
    return jax.shard_map(
        local,
        mesh=mesh,
        in_specs=placed,
        out_specs=(P(("grid", "member"), None), P(("grid", "member")), P(("grid", "member"), None)),
        check_vma=False,
    )
```

profile of v0, /device:TPU:0, one launch (start us, length us, event | category | flops | bytes accessed | tf_op | source)
XLA Modules:
  0.0 299.9 jit_solution(8440790587572666821)
XLA Ops:
  7.2 0.0 copy-start
  7.2 0.0 copy-start.4
  7.2 0.0 copy-start.6
  7.2 0.0 copy-start.5
  7.2 0.0 all-gather.4.cloned.1.call-start
  7.3 1.5 copy-done
  8.8 6.6 %multiply_convert_fusion = (bf16[1024,1024]{1,0:T(8,128)(2,1)S(1)}, f32[1024,1024]{1,0:T(8,128)}) fusion(f32[1024]{0:T(1024)} %param.13, bf16[1024,1024]{1,0:T(8,128)(2,1)} %param.12, bf16[1,1,1024,1024]{3,2,1,0:T(8,128)(2,1)S(1)} %copy-done), kind=kOutput, calls=%fused_computation.8 | convolution fusion | flops 2157969408 | bytes 10489856 | tf_op jit(solution)/shard_map/dot_general | solution.py:24
  15.3 0.0 copy-start.1
  15.3 0.0 copy-start.3
  15.3 0.0 copy-start.7
  15.3 1.4 copy-done.1
  16.7 0.0 copy-done.4
  16.7 0.0 copy-done.6
  16.7 0.0 copy-start.8
  16.7 1.6 convolution_add_fusion
  18.3 0.0 copy-start.2
  18.3 0.0 all-gather.4.cloned.1.call-update
  18.3 0.0 reduce-scatter.7.cloned.1.call-start
  18.3 0.0 copy-done.5
  18.4 66.3 %all-gather.4.cloned.1.call-done = f32[8,100,1024]{2,1,0:T(8,128)} async-done(((f32[1,100,1024]{2,1,0:T(8,128)}), f32[8,100,1024]{2,1,0:T(8,128)}) %all-gather.4.cloned.1.call-update) | async-done | bytes 3276816 | tf_op jit(solution)/shard_map/all_gather | solution.py:43
  84.7 0.0 copy-start.10
  84.7 2.9 multiply_reduce_fusion
  87.6 0.0 copy-done.3
  87.6 0.0 copy-done.7
  87.6 0.0 copy-done.2
  87.6 0.2 multiply_convert_fusion.1
  87.8 0.0 copy-done.8
  87.9 0.2 copy-done.10
  88.0 3.5 %fusion.10 = (f32[1024]{0:T(1024)S(1)}, bf16[1024,1024]{1,0:T(8,128)(2,1)S(1)}) fusion(f32[1024,1024]{1,0:T(8,128)S(1)} %copy-done.10, f32[1024]{0:T(1024)S(1)} %copy-done.8, bf16[100,1024]{1,0:T(8,128)(2,1)S(1)} %multiply_convert_fusion.1, bf16[1024,100]{0,1:T(8,128)(2,1)S(1)} %copy-done.4), kind=kOutput, calls=%fused_computation.19 | convolution fusion | flops 232782848 | bytes 6709248 | tf_op jit(solution)/shard_map/dot_general | solution.py:52
  91.5 4.4 %convolution_bitcast_fusion = f32[1024,1024]{0,1:T(8,128)} fusion(bf16[1,1,1024,1024]{3,2,1,0:T(8,128)(2,1)S(1)} %copy-done, bf16[1024,1024]{1,0:T(8,128)(2,1)S(1)} %get-tuple-element.14), kind=kOutput, calls=%fused_computation.10 | convolution fusion | flops 2147483648 | bytes 8388608 | tf_op jit(solution)/shard_map/dot_general | solution.py:58
  95.9 5.3 %copy.13 = f32[1024,1024]{1,0:T(8,128)} copy(f32[1024,1024]{0,1:T(8,128)} %convolution_bitcast_fusion) | data formatting | bytes 8388608
  101.2 0.0 reduce-scatter.7.cloned.1.call-update
  101.3 0.0 copy-start.9
  101.3 0.0 reduce-scatter.5.cloned.1.call-start
  101.3 3.1 %fusion.11 = f32[1024,100]{1,0:T(8,128)} fusion(bf16[1024,1024]{1,0:T(8,128)(2,1)} %copy-done.1, bf16[100,1024]{1,0:T(8,128)(2,1)S(1)} %multiply_convert_fusion.1), kind=kOutput, calls=%fused_computation.20 | convolution fusion | flops 209715200 | bytes 2711552 | tf_op jit(solution)/shard_map/dot_general | solution.py:62
  104.5 0.0 reduce-scatter.5.cloned.1.call-update
  104.5 0.0 all-reduce.4.cloned.1.call-start
  104.5 92.2 %reduce-scatter.7.cloned.1.call-done = f32[64,1024]{1,0:T(8,128)} async-done(((f32[1024,1024]{1,0:T(8,128)}), f32[64,1024]{1,0:T(8,128)}) %reduce-scatter.7.cloned.1.call-update) | async-done | bytes 262160
  196.7 1.9 copy.14
  198.6 0.0 all-reduce.4.cloned.1.call-update
  198.7 0.0 copy-done.9
  198.7 0.6 dynamic-slice
  199.9 39.2 %all-reduce = f32[1024]{0:T(1024)S(1)} all-reduce(f32[1024]{0:T(1024)S(1)} %get-tuple-element.13), channel_id=4, replica_groups=mesh['grid'=2,'member'=8,'sample'=2] {'grid','member'}, use_global_device_ids=true, to_apply=%region_4.0.clone | all-reduce | flops 1024 | bytes 8192
  239.1 0.1 dynamic-slice.1
  239.2 34.8 %reduce-scatter.5.cloned.1.call-done = f32[64,100]{1,0:T(8,128)} async-done(((f32[1024,100]{1,0:T(8,128)}), f32[64,100]{1,0:T(8,128)}) %reduce-scatter.5.cloned.1.call-update) | async-done | bytes 25616 | tf_op jit(solution)/shard_map/reduce_scatter | solution.py:71
  274.0 4.6 %all-reduce.1 = (f32[64]{0:T(128)}, f32[64,100]{1,0:T(8,128)}) all-reduce(f32[64]{0:T(128)S(1)} %dynamic-slice.1, f32[64,100]{1,0:T(8,128)} %reduce-scatter.5.cloned.1.call-done), channel_id=1, replica_groups=mesh['grid'=2,'member'=8,'sample'=2] {'sample'}, use_global_device_ids=true, to_apply=%region_5.0 | all-reduce | flops 6464 | bytes 51712 | tf_op jit(solution)/shard_map/psum | solution.py:73
  278.6 12.8 %all-reduce.4.cloned.1.call-done = f32[64,1024]{0,1:T(8,128)} async-done(((f32[64,1024]{0,1:T(8,128)}), f32[64,1024]{0,1:T(8,128)}) %all-reduce.4.cloned.1.call-update) | async-done | bytes 262160 | tf_op jit(solution)/shard_map/psum | solution.py:73
  291.5 1.9 copy.12
  (1 shorter events, 0.0 us)
Async XLA Ops:
  7.2 1.6 copy-start
  7.2 9.5 %copy-start.4 = (bf16[1024,100]{0,1:T(8,128)(2,1)S(1)}, bf16[1024,100]{0,1:T(8,128)(2,1)}, u32[]{:S(2)}) copy-start(bf16[1024,100]{0,1:T(8,128)(2,1)} %param.14) | copy-start | bytes 614404
  7.2 9.5 %copy-start.6 = (f32[100]{0:T(128)S(1)}, f32[100]{0:T(128)}, u32[]{:S(2)}) copy-start(f32[100]{0:T(128)} %param.15) | copy-start | bytes 1204
  7.2 11.1 %copy-start.5 = (f32[1024]{0:T(1024)S(1)}, f32[1024]{0:T(1024)}, u32[]{:S(2)}) copy-start(f32[1024]{0:T(1024)} %param.10) | copy-start | bytes 12292
  7.2 77.5 %all-gather.4.cloned.1.call-start = ((), (), s32[]{:S(2)}) async-start(), calls=%async_computation.4 | async-start | bytes 3833856 | tf_op jit(solution)/shard_map/all_gather | solution.py:43
  15.3 1.4 copy-start.1
  15.3 72.3 %copy-start.3 = (f32[1,100,1024]{2,0,1:T(1,128)S(1)}, f32[1,100,1024]{2,0,1:T(1,128)}, u32[]{:S(2)}) copy-start(f32[1,100,1024]{2,0,1:T(1,128)} %param.9) | copy-start | bytes 1228804
  15.3 72.3 %copy-start.7 = (f32[100]{0:T(128)S(1)}, f32[100]{0:T(128)}, u32[]{:S(2)}) copy-start(f32[100]{0:T(128)} %param.11) | copy-start | bytes 1204
  16.7 71.1 %copy-start.8 = (f32[1024]{0:T(1024)S(1)}, f32[1024]{0:T(1024)}, u32[]{:S(2)}) copy-start(f32[1024]{0:T(1024)} %param.13) | copy-start | bytes 12292
  18.3 69.3 %copy-start.2 = (f32[1024,100]{0,1:T(8,128)S(1)}, f32[1024,100]{0,1:T(8,128)}, u32[]{:S(2)}) copy-start(f32[1024,100]{0,1:T(8,128)} %convolution_add_fusion) | copy-start | bytes 1228804
  18.3 178.4 %reduce-scatter.7.cloned.1.call-start = ((), (), s32[]{:S(2)}) async-start(), calls=%async_computation.5 | async-start | bytes 4456448
  84.7 3.3 %copy-start.10 = (f32[1024,1024]{1,0:T(8,128)S(1)}, f32[1024,1024]{1,0:T(8,128)}, u32[]{:S(2)}) copy-start(f32[1024,1024]{1,0:T(8,128)} %get-tuple-element.12) | copy-start | bytes 12582916
  101.3 97.4 %copy-start.9 = (u32[32]{0:T(128)S(1)}, u32[32]{0:T(128)}, u32[]{:S(2)}) copy-start(u32[32]{0:T(128)} %constant.27) | copy-start | bytes 388
  101.3 172.7 %reduce-scatter.5.cloned.1.call-start = ((), (), s32[]{:S(2)}) async-start(), calls=%async_computation.3 | async-start | bytes 557056 | tf_op jit(solution)/shard_map/reduce_scatter | solution.py:71
  104.5 187.0 %all-reduce.4.cloned.1.call-start = ((), (), s32[]{:S(2)}) async-start(), calls=%async_computation.2 | async-start | bytes 1048576 | tf_op jit(solution)/shard_map/psum | solution.py:73
Sparse Core Ops, SparseCore 0:
  18.4 66.2 all-gather.3
  101.4 95.2 reduce-scatter.6
  198.9 75.0 reduce-scatter.4
  276.3 15.0 all-reduce.3
where the time goes:
time: 300 us
  waiting for transfers between devices  206 us (69%)
  blocking collectives  43.9 us (15%)
  matrix products  19.1 us (6%)
  between operations  14.5 us (5%)
  local copies, waits for them, and re-layouts  13 us (4%)
  other arithmetic  3.12 us (1%)
    unnamed x5, waiting for transfers between devices  92.2 us
    all_gather x1, waiting for transfers between devices, local(): lax.all_gather(member_prediction[None], 'member', axis=0, tiled=True)  66.3 us
    unnamed x1, blocking collectives  39.2 us
    reduce_scatter x1, waiting for transfers between devices, local(): lax.psum_scatter(grad_out, ('grid', 'member'), scatter_dimension=0, tiled...  34.8 us
    unnamed x27, local copies, waits for them, and re-layouts  13 us
    psum x1, waiting for transfers between devices, local(): totals = lax.psum((shares[0], shares[1], shares[2]), 'sample')  12.8 us
    dot_general x1, matrix products, local(): jnp.dot(inputs, weight_in, preferred_element_type=jnp.float32) + bias_in  6.58 us
  transfers between devices with their start and end apart: 4, of which 4 were waited for; matrix products, arithmetic and copies ran while one was open for 2% of the time, Pallas kernels for 0%

commit v1 on v0

v1 whole, which is shorter than its diff:
```python
import functools
import math

import jax
import jax.numpy as jnp
from jax import lax
from jax.experimental import pallas as pl
from jax.experimental.pallas import tpu as pltpu
from jax.sharding import PartitionSpec as P

smoothing = 0.01
alpha_fair = 0.95
LANES = 128
MEMBER_ROWS = 4
GELU_C = math.sqrt(2.0 / math.pi)
GELU_A = 0.044715
MESH = pl.DeviceIdType.MESH
F32 = jnp.float32
BF16 = jnp.bfloat16
ORDERS = ("xyz", "yxz", "xyz", "yxz", "yxz")


def softened_slope(value):
    return value * lax.rsqrt(value * value + smoothing)


def kernel(
    sizes, chunk_axes,
    x_hbm, t_hbm, area_ref, var_ref, win_hbm, bin_ref, wout_hbm, bout_ref,
    gin_ref, gbias_ref, gout_ref,
    x_v, xt_v, win_v, wout_v, w128, w128t, tv, t128, tt,
    pre, act, pg, bias_acc, fsend, frecv, gsend, grecv, goutt,
    csend, crecv, own, s1, r1, s2, r2, s3, r3, acc, fin_s, fin_r,
    in_sem, f_ss, f_rs, g_ss, g_rs, c_ss, c_rs, r_ss, r_rs, e_ss, e_rs,
):
    G, MZ, MX, S, R = sizes
    M = MZ * MX
    points, depth = x_v.shape
    width = win_v.shape[1]
    fields = wout_v.shape[1]
    per = points // M
    step = points // MZ
    half = width // S
    grid = lax.axis_index("grid")
    me = lax.axis_index("member")
    core = lax.axis_index("sample")
    mz, mx = me // MX, me % MX
    other = 1 - core

    pending = []

    def fetch(src, dst, n):
        copy = pltpu.make_async_copy(src, dst, in_sem.at[n])
        copy.start()
        return copy

    def rows_of(i):
        return pl.multiple_of(lax.rem(mz + 1 + i, MZ) * step, step)

    get_win = fetch(win_hbm, win_v, 0)
    get_x = [
        fetch(x_hbm.at[0, 0, pl.ds(rows_of(i), step)], x_v.at[pl.ds(rows_of(i), step)], 1 + i)
        for i in range(MZ)
    ]
    get_wout = fetch(wout_hbm, wout_v, 1 + MZ)
    get_t = fetch(t_hbm.at[0], tv, 2 + MZ)

    barrier = pltpu.get_barrier_semaphore()
    for s in range(1, M):
        pl.semaphore_signal(barrier, inc=1, device_id={"member": lax.rem(me + s, M)}, device_id_type=MESH)
    for s in range(1, G):
        pl.semaphore_signal(barrier, inc=1, device_id={"grid": lax.rem(grid + s, G)}, device_id_type=MESH)
    pl.semaphore_signal(barrier, inc=1, device_id={"sample": other}, device_id_type=MESH)

    w128[...] = jnp.zeros_like(w128)
    get_wout.wait()
    w128[:, 0:fields] = wout_v[...]
    get_win.wait()

    def remote(src, dst, ss, rs, axis, index):
        return pltpu.make_async_remote_copy(
            src_ref=src, dst_ref=dst, send_sem=ss, recv_sem=rs,
            device_id={axis: index}, device_id_type=MESH,
        )

    f_copies = []
    for i in range(MZ):
        base = rows_of(i)
        get_x[i].wait()
        pre[pl.ds(base, step)] = jnp.dot(
            x_v[pl.ds(base, step)], win_v[...], preferred_element_type=F32
        )

        @pl.loop(0, step // 16)
        def _(n):
            at = pl.ds(pl.multiple_of(base + n * 16, 16), 16)
            z = pre[at] + bin_ref[...]
            pre[at] = z
            t = jnp.tanh(z * (GELU_C + (GELU_C * GELU_A) * (z * z)))
            hz = 0.5 * z
            act[at] = (hz + hz * t).astype(BF16)

        value = jnp.dot(act[pl.ds(base, step)], w128[...], preferred_element_type=F32)
        zq = lax.rem(mz + 1 + i, MZ)
        fsend[pl.ds(zq * MX, MX)] = value.reshape(MX, per, LANES).astype(BF16)
        if i == 0:
            pl.semaphore_wait(barrier, (M - 1) + (G - 1) + 1)
        for o in range(MX):
            if i == MZ - 1 and o == 0:
                continue
            j = zq * MX + lax.rem(mx + o, MX)
            copy = remote(
                fsend.at[j], frecv.at[me], f_ss.at[i * MX + o], f_rs.at[i * MX + o], "member", j
            )
            copy.start()
            f_copies.append(copy)
    frecv[pl.ds(me, 1)] = fsend[pl.ds(me, 1)]

    get_t.wait()
    t128[...] = jnp.zeros_like(t128)
    t128[0:fields] = tv[...]
    t128[fields : fields + 1] = area_ref[...]
    tt[...] = t128[...].T
    bout = jnp.concatenate([bout_ref[...], jnp.zeros((1, LANES - fields), F32)], axis=1)
    var = jnp.concatenate([var_ref[...], jnp.zeros((1, LANES - fields), F32)], axis=1)
    eps_fair = (1.0 - alpha_fair) / M
    pairwise = (1.0 - eps_fair) / (M * (M - 1))
    loss_scale = M / math.sqrt(S * G * points)

    for copy in f_copies:
        copy.wait_recv()

    @pl.loop(0, per // 16)
    def _(n):
        at = pl.ds(pl.multiple_of(n * 16, 16), 16)
        seen = tt[pl.ds(pl.multiple_of(me * per + n * 16, 16), 16)]
        scale = (loss_scale * seen[:, fields : fields + 1]) * var
        target = seen - bout
        f = [frecv[j, at].astype(F32) for j in range(M)]
        total = [jnp.zeros((16, LANES), F32) for _ in range(M)]
        for j in range(M):
            for k in range(j + 1, M):
                slope = softened_slope(f[j] - f[k])
                total[j] = total[j] + slope
                total[k] = total[k] - slope
        for j in range(M):
            g = scale * (softened_slope(f[j] - target) * (1.0 / M) - pairwise * total[j])
            gsend[j, at] = g.astype(BF16)

    g_copies = {}
    for i in (1, 2, 0, 3):
        zq = lax.rem(mz + 1 + i, MZ)
        for o in range(MX):
            if i == MZ - 1 and o == 0:
                continue
            j = zq * MX + lax.rem(mx + o, MX)
            copy = remote(
                gsend.at[j], grecv.at[me], g_ss.at[i * MX + o], g_rs.at[i * MX + o], "member", j
            )
            copy.start()
            g_copies[(i, o)] = copy
    grecv[pl.ds(me, 1)] = gsend[pl.ds(me, 1)]

    @pl.loop(0, points // 16)
    def _(n):
        at = pl.ds(pl.multiple_of(n * 16, 16), 16)
        z = pre[at]
        q = z * z
        t = jnp.tanh(z * (GELU_C + (GELU_C * GELU_A) * q))
        inner = GELU_C + (3.0 * GELU_C * GELU_A) * q
        pre[at] = (0.5 + 0.5 * t) + (0.5 * z) * (1.0 - t * t) * inner

    w128t[...] = w128[...].T
    for n in range(points // 256):
        xt_v[:, n * 256 : (n + 1) * 256] = x_v[n * 256 : (n + 1) * 256, :].T
    bias_acc[...] = jnp.zeros_like(bias_acc)

    for i in (3, 0, 2, 1):
        for o in range(MX):
            if (i, o) in g_copies:
                g_copies[(i, o)].wait_recv()
        zq = lax.rem(mz + 2 * MZ - 1 - i, MZ)
        base = pl.multiple_of(zq * step, step)
        rows = grecv[pl.ds(zq * MX, MX)].reshape(step, LANES)
        back = jnp.dot(rows, w128t[...], preferred_element_type=F32)
        pre[pl.ds(base, step)] = pre[pl.ds(base, step)] * back

        @pl.loop(0, step // 16)
        def _(n):
            at = pl.ds(pl.multiple_of(base + n * 16, 16), 16)
            value = pre[at]
            pg[at] = value.astype(BF16)
            bias_acc[...] += value[0:8] + value[8:16]

    goutt[...] = lax.dot_general(
        grecv[...].reshape(points, LANES), act[...], (((0,), (0,)), ((), ())),
        preferred_element_type=F32,
    )
    goutt[fields : fields + 1] = jnp.sum(bias_acc[...], axis=0, keepdims=True)
    chunks = half // LANES
    blocks = (G, MZ, MX, R, LANES)
    last = chunks
    kind = csend.dtype
    csend[last] = goutt[...].T.reshape(blocks).astype(kind)

    c_copies = []

    def exchange(n):
        copy = remote(csend.at[n], crecv.at[n], c_ss.at[n], c_rs.at[n], "sample", other)
        copy.start()
        c_copies.append(copy)

    exchange(last)
    per_dot = 2
    wide = per_dot * LANES
    for n in range(0, chunks, per_dot):
        at = pl.ds(pl.multiple_of(other * half + n * LANES, LANES), wide)
        value = jnp.dot(xt_v[...], pg[:, at], preferred_element_type=F32)
        for u in range(per_dot):
            csend[n + u] = value[:, u * LANES : (u + 1) * LANES].reshape(blocks).astype(kind)
            exchange(n + u)

    lengths = {"x": MX, "y": G, "z": MZ}
    index = {"x": mx, "y": grid, "z": mz}
    sem_base = {}
    sem_count = 0
    for n in range(chunks + 1):
        for stage in range(3):
            sem_base[(n, stage)] = sem_count
            sem_count += lengths[chunk_axes[n][stage]] - 1
    live = {}

    def peer(axis, to):
        if axis == "y":
            return "grid", to
        if axis == "x":
            return "member", mz * MX + to
        return "member", to * MX + mx

    def part(ref, axes, axis, to):
        where = [slice(None)] * len(axes)
        where[axes.index(axis)] = to
        return ref.at[tuple(where)]

    def send(n, stage, src, dst, axes):
        axis = chunk_axes[n][stage]
        started = []
        for s in range(1, lengths[axis]):
            to = lax.rem(index[axis] + s, lengths[axis])
            name, where = peer(axis, to)
            sem = sem_base[(n, stage)] + s - 1
            copy = remote(
                part(src, axes, axis, to), dst.at[s - 1], r_ss.at[sem], r_rs.at[sem], name, where
            )
            copy.start()
            started.append(copy)
        live[(n, stage)] = started

    def first(n):
        c_copies_of[n].wait_recv()
        if n == last:
            total = csend[n].astype(F32) + crecv[n].astype(F32)
        else:
            total = own[n] + crecv[n].astype(F32)
            own[n] = total
        s1[n] = total.astype(kind)
        send(n, 0, s1.at[n], r1[n], "yzx")

    def arrived(n, stage, kept, source):
        total = kept
        for s, copy in enumerate(live[(n, stage)]):
            copy.wait_recv()
            total = total + source[s].astype(F32)
        return total

    def second(n):
        axis = chunk_axes[n][0]
        source = s1.at[n] if n == last else own.at[n]
        kept = part(source, "yzx", axis, index[axis])[...].astype(F32)
        total = arrived(n, 0, kept, r1[n])
        acc[0][n][...] = total
        s2[n][...] = total.astype(kind)
        send(n, 1, s2[n], r2[n], "yzx".replace(axis, ""))

    def third(n):
        axes = "yzx".replace(chunk_axes[n][0], "")
        axis = chunk_axes[n][1]
        kept = part(acc[0][n], axes, axis, index[axis])[...]
        total = arrived(n, 1, kept, r2[n])
        acc[1][n][...] = total
        s3[n][...] = total.astype(kind)
        send(n, 2, s3[n], r3[n], axes.replace(axis, ""))

    e_copies = []

    def finish(n):
        axis = chunk_axes[n][2]
        total = arrived(n, 2, acc[1][n][index[axis]], r3[n])
        if n == last:
            gout_ref[...] = total[:, 0:fields]
            gbias_ref[...] = total.T[fields : fields + 1, :]
            return
        fin_s[n] = total
        copy = remote(fin_s.at[n], fin_r.at[n], e_ss.at[n], e_rs.at[n], "sample", other)
        copy.start()
        e_copies.append(copy)
        at = pl.ds(pl.multiple_of(core * half + n * LANES, LANES), LANES)
        gin_ref[:, at] = total

    c_copies_of = dict(zip([last] + list(range(chunks)), c_copies))
    first(last)
    for n in range(0, chunks, per_dot):
        at = pl.ds(pl.multiple_of(core * half + n * LANES, LANES), wide)
        value = jnp.dot(xt_v[...], pg[:, at], preferred_element_type=F32)
        for u in range(per_dot):
            own[n + u] = value[:, u * LANES : (u + 1) * LANES].reshape(blocks)
            first(n + u)
    order = [last] + list(range(chunks))
    plan = []
    for place, n in enumerate(order):
        plan.append((place, 0, second, n))
        plan.append((place + 2, 1, third, n))
        plan.append((place + 4, 2, finish, n))
    plan.sort(key=lambda entry: entry[:2])
    for _, _, act_on, n in plan:
        act_on(n)
    for n in range(chunks):
        e_copies[n].wait_recv()
        at = pl.ds(pl.multiple_of(other * half + n * LANES, LANES), LANES)
        gin_ref[:, at] = fin_r[n]

    for copy in f_copies + list(g_copies.values()) + c_copies + e_copies:
        copy.wait_send()
    for started in live.values():
        for copy in started:
            copy.wait_send()


def local(
    sizes, hidden_states, targets, area_weight, var_weight, weight_in, bias_in, output_weight,
    output_bias,
):
    G, M, S = sizes
    MZ = MEMBER_ROWS
    MX = M // MZ
    points, depth = hidden_states.shape[2:]
    width, fields = output_weight.shape
    R = width // (G * M)
    per = points // M
    kind = BF16 if R % 16 == 0 else F32
    chunks = width // S // LANES
    chunk_axes = [ORDERS[n % 4] for n in range(chunks)] + [ORDERS[4]]
    lengths = {"x": MX, "y": G, "z": MZ}

    def dims(axes):
        return tuple(lengths[a] for a in axes)

    r1, s2, r2, a2, s3, r3, a3 = [], [], [], [], [], [], []
    sems = 0
    for axes in chunk_axes:
        rest = "yzx".replace(axes[0], "")
        one = rest.replace(axes[1], "")
        r1.append(pltpu.VMEM((lengths[axes[0]] - 1, *dims(rest), R, LANES), kind))
        s2.append(pltpu.VMEM((*dims(rest), R, LANES), kind))
        a2.append(pltpu.VMEM((*dims(rest), R, LANES), F32))
        r2.append(pltpu.VMEM((lengths[axes[1]] - 1, *dims(one), R, LANES), kind))
        s3.append(pltpu.VMEM((*dims(one), R, LANES), kind))
        a3.append(pltpu.VMEM((*dims(one), R, LANES), F32))
        r3.append(pltpu.VMEM((lengths[axes[2]] - 1, R, LANES), kind))
        sems += sum(lengths[a] - 1 for a in axes)
    blocks = (G, MZ, MX, R, LANES)
    dma = pltpu.SemaphoreType.DMA
    scratch = [
        pltpu.VMEM((points, depth), BF16),
        pltpu.VMEM((depth, points), BF16),
        pltpu.VMEM((depth, width), BF16),
        pltpu.VMEM((width, fields), BF16),
        pltpu.VMEM((width, LANES), BF16),
        pltpu.VMEM((LANES, width), BF16),
        pltpu.VMEM((fields, points), F32),
        pltpu.VMEM((LANES, points), F32),
        pltpu.VMEM((points, LANES), F32),
        pltpu.VMEM((points, width), F32),
        pltpu.VMEM((points, width), BF16),
        pltpu.VMEM((points, width), BF16),
        pltpu.VMEM((8, width), F32),
        pltpu.VMEM((M, per, LANES), BF16),
        pltpu.VMEM((M, per, LANES), BF16),
        pltpu.VMEM((M, per, LANES), BF16),
        pltpu.VMEM((M, per, LANES), BF16),
        pltpu.VMEM((LANES, width), F32),
        pltpu.VMEM((chunks + 1, *blocks), kind),
        pltpu.VMEM((chunks + 1, *blocks), kind),
        pltpu.VMEM((chunks, *blocks), F32),
        pltpu.VMEM((chunks + 1, *blocks), kind),
        r1, s2, r2, s3, r3, [a2, a3],
        pltpu.VMEM((chunks, R, LANES), F32),
        pltpu.VMEM((chunks, R, LANES), F32),
        dma((3 + MZ,)), dma((M,)), dma((M,)), dma((M,)), dma((M,)),
        dma((chunks + 1,)), dma((chunks + 1,)), dma((sems,)), dma((sems,)),
        dma((chunks,)), dma((chunks,)),
    ]
    flat, tree = jax.tree.flatten(scratch, is_leaf=lambda leaf: not isinstance(leaf, list))

    def body(*refs):
        head, tail = refs[:11], refs[11:]
        kernel(
            (G, MZ, MX, S, R), chunk_axes, *head, *jax.tree.unflatten(tree, tail)
        )

    whole = pl.BlockSpec(memory_space=pltpu.VMEM)
    anywhere = pl.BlockSpec(memory_space=pl.ANY)
    flops = 4 * points * depth * width + 6 * points * width * LANES
    gin, gbias, gout = pl.pallas_call(
        body,
        out_shape=(
            jax.ShapeDtypeStruct((R, width), F32),
            jax.ShapeDtypeStruct((1, R), F32),
            jax.ShapeDtypeStruct((R, fields), F32),
        ),
        in_specs=[anywhere, anywhere, whole, whole, anywhere, whole, anywhere, whole],
        out_specs=(whole, whole, whole),
        scratch_shapes=flat,
        compiler_params=pltpu.CompilerParams(
            collective_id=0, has_side_effects=True, vmem_limit_bytes=56 * 1024 * 1024
        ),
        cost_estimate=pl.CostEstimate(
            flops=flops, bytes_accessed=6 * 1024 * 1024, transcendentals=2 * points * width
        ),
        name="crps_gradient",
    )(
        hidden_states, targets, area_weight[None], var_weight[None], weight_in, bias_in[None],
        output_weight, output_bias[None],
    )
    return gin, gbias.reshape(R), gout


def solution(mesh):
    placed = (
        P("sample", "member", "grid", None),
        P("sample", None, "grid"),
        P("grid"),
        P(),
        P(),
        P(),
        P(),
        P(),
    )
    sizes = (mesh.shape["grid"], mesh.shape["member"], mesh.shape["sample"])
    return jax.shard_map(
        functools.partial(local, sizes),
        mesh=mesh,
        in_specs=placed,
        out_specs=(P(("grid", "member"), None), P(("grid", "member")), P(("grid", "member"), None)),
        check_vma=False,
    )
```

time: 300 us -> 59.5 us (0.20)
  waiting for transfers between devices: 206 us -> 0 us
  Pallas kernels: 0 us -> 50.7 us
  blocking collectives: 43.9 us -> 0 us
  matrix products: 19.1 us -> 0 us
  between operations: 14.5 us -> 0.64 us
  local copies, waits for them, and re-layouts: 13 us -> 7.79 us
  other arithmetic: 3.12 us -> 0 us
    unnamed x5 -> x0, waiting for transfers between devices: 92.2 us -> none
    all_gather x1 -> x0, waiting for transfers between devices: 66.3 us -> none  [local(): lax.all_gather(member_prediction[None], 'member', axis=0, tiled=True)]
    pallas_call x0 -> x1, Pallas kernels: none -> 50.7 us  [local(): pl.pallas_call(body, out_shape=(jax.ShapeDtypeStruct((R, width), F32), ja...]
    unnamed x1 -> x0, blocking collectives: 39.2 us -> none
    reduce_scatter x1 -> x0, waiting for transfers between devices: 34.8 us -> none  [local(): lax.psum_scatter(grad_out, ('grid', 'member'), scatter_dimension=0, tiled...]
    dot_general x5 -> x0, matrix products: 19.1 us -> none  [the longest x1 6.58 us: local(): jnp.dot(inputs, weight_in, preferred_element_type=jnp.float32) + bias_in]
    psum x1 -> x0, waiting for transfers between devices: 12.8 us -> none  [local(): totals = lax.psum((shares[0], shares[1], shares[2]), 'sample')]
    unnamed x27 -> x5, local copies, waits for them, and re-layouts: 13 us -> 7.79 us
  transfers between devices with their start and end apart: 4 -> 0, of which waited for: 4 -> 0; matrix products, arithmetic and copies ran while one was open for 2% -> 0% of each run, Pallas kernels for 0% -> 0%
where the time goes in v1:
time: 59.5 us; the launch traced here: 59.1 us
  Pallas kernels  50.7 us (85%)
  local copies, waits for them, and re-layouts  7.79 us (13%)
  between operations  0.64 us (1%)
    pallas_call x1, Pallas kernels, local(): pl.pallas_call(body, out_shape=(jax.ShapeDtypeStruct((R, width), F32), ja...  50.7 us
    unnamed x5, local copies, waits for them, and re-layouts  7.79 us

profile of v1, /device:TPU:0, one launch (start us, length us, event | category | flops | bytes accessed | tf_op | source)
XLA Modules:
  0.0 59.1 jit_solution(11099450336691684320)
XLA Ops:
  0.6 1.8 %copy.12.refs_6_ = bf16[1024,100]{1,0:T(8,128)(2,1)} copy(bf16[1024,100]{0,1:T(8,128)(2,1)} %param.14) | data formatting | bytes 409600 | tf_op args[6]
  2.4 1.8 %copy.11.refs_1_ = f32[1,100,1024]{2,1,0:T(8,128)} copy(f32[1,100,1024]{2,0,1:T(1,128)} %param.9) | data formatting | bytes 819200 | tf_op args[1]
  4.3 50.7 %crps_gradient.1 = (f32[64,1024]{1,0:T(8,128)}, f32[1,64]{1,0:T(1,128)}, f32[64,100]{1,0:T(8,128)}) custom-call(bf16[1,1,1024,1024]{3,2,1,0:T(8,128)(2,1)} %refs_0_.1, f32[1,100,1024]{2,1,0:T(8,128)} %copy.11.refs_1_, f32[1,1024]{1,0:T(1,128)} %bitcast.5, f32[1,100]{1,0:T(1,128)} %bitcast.7, bf16[1024,1024]{1,0:T(8,128)(2,1)} %refs_4_.1, f32[1,1024]{1,0:T(1,128)} %bitcast.6, ...), custom_call_target="tpu_custom_call" | custom-call | flops 5100273664 | bytes 6291456 | tf_op jit(solution)/shard_map/crps_gradient/pallas_call | solution.py:414
  55.0 1.7 %copy.16 = f32[64,1024]{1,0:T(8,128)} copy(f32[64,1024]{1,0:T(8,128)} %get-tuple-element.12) | data formatting | bytes 524288
  56.6 1.1 %copy.17 = f32[64]{0:T(128)} copy(f32[64]{0:T(128)} %bitcast.9) | data formatting | bytes 512
  57.8 1.4 %copy.18 = f32[64,100]{1,0:T(8,128)} copy(f32[64,100]{1,0:T(8,128)} %get-tuple-element.14) | data formatting | bytes 51200

commit v2 on v1

--- a/solution.py
+++ b/solution.py
@@ -17,7 +17,8 @@
 MESH = pl.DeviceIdType.MESH
 F32 = jnp.float32
 BF16 = jnp.bfloat16
-ORDERS = ("xyz", "yxz", "xyz", "yxz", "yxz")
+ORDERS = ("xzy", "yzx", "xyz", "yxz", "zxy")
+PLAN = ((0, 0), (0, 1), (0, 4), (0, 2), (0, 3), (1, 0), (1, 1), (1, 4), (1, 2), (1, 3))
 
 
 def softened_slope(value):
@@ -28,16 +29,17 @@
     sizes, chunk_axes,
     x_hbm, t_hbm, area_ref, var_ref, win_hbm, bin_ref, wout_hbm, bout_ref,
     gin_ref, gbias_ref, gout_ref,
-    x_v, xt_v, win_v, wout_v, w128, w128t, tv, t128, tt,
+    x_v, xt_v, win_v, wout_v, w128, w128t, tv, tt,
     pre, act, pg, bias_acc, fsend, frecv, gsend, grecv, goutt,
-    csend, crecv, own, s1, r1, s2, r2, s3, r3, acc, fin_s, fin_r,
+    csend, crecv, own, o_all, o_fin, s1, r1, s2, r2, s3, r3, acc, fin_s, fin_r,
     in_sem, f_ss, f_rs, g_ss, g_rs, c_ss, c_rs, r_ss, r_rs, e_ss, e_rs,
 ):
     G, MZ, MX, S, R = sizes
     M = MZ * MX
     points, depth = x_v.shape
     width = win_v.shape[1]
-    fields = wout_v.shape[1]
+    fields = wout_v.shape[0]
+    tiles = tv.shape[0]
     per = points // M
     step = points // MZ
     half = width // S
@@ -63,7 +65,8 @@
         for i in range(MZ)
     ]
     get_wout = fetch(wout_hbm, wout_v, 1 + MZ)
-    get_t = fetch(t_hbm.at[0], tv, 2 + MZ)
+    tile = (me * per) // LANES
+    get_t = [fetch(t_hbm.at[:, tile + n], tv.at[n], 2 + MZ + n) for n in range(tiles)]
 
     barrier = pltpu.get_barrier_semaphore()
     for s in range(1, M):
@@ -72,9 +75,10 @@
         pl.semaphore_signal(barrier, inc=1, device_id={"grid": lax.rem(grid + s, G)}, device_id_type=MESH)
     pl.semaphore_signal(barrier, inc=1, device_id={"sample": other}, device_id_type=MESH)
 
-    w128[...] = jnp.zeros_like(w128)
+    w128t[...] = jnp.zeros_like(w128t)
     get_wout.wait()
-    w128[:, 0:fields] = wout_v[...]
+    w128t[0:fields] = wout_v[...]
+    w128[...] = w128t[...].T
     get_win.wait()
 
     def remote(src, dst, ss, rs, axis, index):
@@ -116,11 +120,13 @@
             f_copies.append(copy)
     frecv[pl.ds(me, 1)] = fsend[pl.ds(me, 1)]
 
-    get_t.wait()
-    t128[...] = jnp.zeros_like(t128)
-    t128[0:fields] = tv[...]
-    t128[fields : fields + 1] = area_ref[...]
-    tt[...] = t128[...].T
+    for n in range(tiles):
+        get_t[n].wait()
+        rest = jnp.zeros((LANES - fields - 1, LANES), F32)
+        tt[n * LANES : (n + 1) * LANES] = jnp.concatenate(
+            [tv[n], area_ref[pl.ds(tile + n, 1)], rest], axis=0
+        ).T
+    shift = me * per - tile * LANES
     bout = jnp.concatenate([bout_ref[...], jnp.zeros((1, LANES - fields), F32)], axis=1)
     var = jnp.concatenate([var_ref[...], jnp.zeros((1, LANES - fields), F32)], axis=1)
     eps_fair = (1.0 - alpha_fair) / M
@@ -133,7 +139,7 @@
     @pl.loop(0, per // 16)
     def _(n):
         at = pl.ds(pl.multiple_of(n * 16, 16), 16)
-        seen = tt[pl.ds(pl.multiple_of(me * per + n * 16, 16), 16)]
+        seen = tt[pl.ds(pl.multiple_of(shift + n * 16, 16), 16)]
         scale = (loss_scale * seen[:, fields : fields + 1]) * var
         target = seen - bout
         f = [frecv[j, at].astype(F32) for j in range(M)]
@@ -170,7 +176,6 @@
         inner = GELU_C + (3.0 * GELU_C * GELU_A) * q
         pre[at] = (0.5 + 0.5 * t) + (0.5 * z) * (1.0 - t * t) * inner
 
-    w128t[...] = w128[...].T
     for n in range(points // 256):
         xt_v[:, n * 256 : (n + 1) * 256] = x_v[n * 256 : (n + 1) * 256, :].T
     bias_acc[...] = jnp.zeros_like(bias_acc)
@@ -198,28 +203,11 @@
     )
     goutt[fields : fields + 1] = jnp.sum(bias_acc[...], axis=0, keepdims=True)
     chunks = half // LANES
+    last = chunks
+    kind = s1[0].dtype
+    split = o_fin.shape[1] < R
     blocks = (G, MZ, MX, R, LANES)
-    last = chunks
-    kind = csend.dtype
-    csend[last] = goutt[...].T.reshape(blocks).astype(kind)
-
-    c_copies = []
-
-    def exchange(n):
-        copy = remote(csend.at[n], crecv.at[n], c_ss.at[n], c_rs.at[n], "sample", other)
-        copy.start()
-        c_copies.append(copy)
-
-    exchange(last)
-    per_dot = 2
-    wide = per_dot * LANES
-    for n in range(0, chunks, per_dot):
-        at = pl.ds(pl.multiple_of(other * half + n * LANES, LANES), wide)
-        value = jnp.dot(xt_v[...], pg[:, at], preferred_element_type=F32)
-        for u in range(per_dot):
-            csend[n + u] = value[:, u * LANES : (u + 1) * LANES].reshape(blocks).astype(kind)
-            exchange(n + u)
-
+    o_all[...] = goutt[...].T.reshape(o_all.shape)
     lengths = {"x": MX, "y": G, "z": MZ}
     index = {"x": mx, "y": grid, "z": mz}
     sem_base = {}
@@ -256,15 +244,33 @@
             started.append(copy)
         live[(n, stage)] = started
 
+    c_copies = {}
+
+    def exchange(n):
+        copy = remote(csend[n], crecv[n], c_ss.at[n], c_rs.at[n], "sample", other)
+        copy.start()
+        c_copies[n] = copy
+
+    def columns(n, owner):
+        at = pl.ds(pl.multiple_of(owner * half + n * LANES, LANES), 2 * LANES)
+        value = jnp.dot(xt_v[...], pg[:, at], preferred_element_type=F32)
+        return [value[:, u * LANES : (u + 1) * LANES].reshape(blocks) for u in range(2)]
+
+    def give(n):
+        for u, value in enumerate(columns(n, other)):
+            csend[n + u][...] = value.astype(kind)
+            exchange(n + u)
+
+    def keep(n):
+        for u, value in enumerate(columns(n, core)):
+            own[n + u][...] = value
+
     def first(n):
-        c_copies_of[n].wait_recv()
-        if n == last:
-            total = csend[n].astype(F32) + crecv[n].astype(F32)
-        else:
-            total = own[n] + crecv[n].astype(F32)
-            own[n] = total
-        s1[n] = total.astype(kind)
-        send(n, 0, s1.at[n], r1[n], "yzx")
+        c_copies[n].wait_recv()
+        total = own[n][...] + crecv[n][...].astype(F32)
+        own[n][...] = total
+        s1[n][...] = total.astype(kind)
+        send(n, 0, s1[n], r1[n], "yzx")
 
     def arrived(n, stage, kept, source):
         total = kept
@@ -275,8 +281,7 @@
 
     def second(n):
         axis = chunk_axes[n][0]
-        source = s1.at[n] if n == last else own.at[n]
-        kept = part(source, "yzx", axis, index[axis])[...].astype(F32)
+        kept = part(own[n], "yzx", axis, index[axis])[...]
         total = arrived(n, 0, kept, r1[n])
         acc[0][n][...] = total
         s2[n][...] = total.astype(kind)
@@ -291,49 +296,75 @@
         s3[n][...] = total.astype(kind)
         send(n, 2, s3[n], r3[n], axes.replace(axis, ""))
 
-    e_copies = []
+    e_copies = {}
 
     def finish(n):
         axis = chunk_axes[n][2]
         total = arrived(n, 2, acc[1][n][index[axis]], r3[n])
         if n == last:
-            gout_ref[...] = total[:, 0:fields]
-            gbias_ref[...] = total.T[fields : fields + 1, :]
-            return
-        fin_s[n] = total
-        copy = remote(fin_s.at[n], fin_r.at[n], e_ss.at[n], e_rs.at[n], "sample", other)
+            o_fin[core if split else 0] = total
+            if not split:
+                return
+        else:
+            at = pl.ds(pl.multiple_of(core * half + n * LANES, LANES), LANES)
+            gin_ref[:, at] = total
+        fin_s[n][...] = total
+        copy = remote(fin_s[n], fin_r[n], e_ss.at[n], e_rs.at[n], "sample", other)
         copy.start()
-        e_copies.append(copy)
-        at = pl.ds(pl.multiple_of(core * half + n * LANES, LANES), LANES)
-        gin_ref[:, at] = total
-
-    c_copies_of = dict(zip([last] + list(range(chunks)), c_copies))
-    first(last)
-    for n in range(0, chunks, per_dot):
-        at = pl.ds(pl.multiple_of(core * half + n * LANES, LANES), wide)
-        value = jnp.dot(xt_v[...], pg[:, at], preferred_element_type=F32)
-        for u in range(per_dot):
-            own[n + u] = value[:, u * LANES : (u + 1) * LANES].reshape(blocks)
-            first(n + u)
-    order = [last] + list(range(chunks))
-    plan = []
-    for place, n in enumerate(order):
-        plan.append((place, 0, second, n))
-        plan.append((place + 2, 1, third, n))
-        plan.append((place + 4, 2, finish, n))
-    plan.sort(key=lambda entry: entry[:2])
-    for _, _, act_on, n in plan:
-        act_on(n)
+        e_copies[n] = copy
+
+    left = set()
+
+    def gone(n, stage):
+        for copy in live[(n, stage)]:
+            copy.wait_send()
+        left.add((n, stage))
+
+    give(0)
+    if split:
+        csend[last][...] = o_all[:, :, :, other].astype(kind)
+        own[last][...] = o_all[:, :, :, core]
+    else:
+        csend[last][...] = o_all[:, :, :, 0].astype(kind)
+        own[last][...] = csend[last][...].astype(F32)
+    exchange(last)
+    keep(0)
+    for n in (0, 1, last):
+        first(n)
+    for n in range(2, chunks, 2):
+        give(n)
+        keep(n)
+    for n in range(2, chunks):
+        gone(n - 2, 0)
+        first(n)
+    for stage, n in PLAN:
+        (second, third)[stage](n)
+    for n in (last, *range(chunks)):
+        finish(n)
     for n in range(chunks):
         e_copies[n].wait_recv()
         at = pl.ds(pl.multiple_of(other * half + n * LANES, LANES), LANES)
-        gin_ref[:, at] = fin_r[n]
-
-    for copy in f_copies + list(g_copies.values()) + c_copies + e_copies:
+        gin_ref[:, at] = fin_r[n][...]
+    if split:
+        e_copies[last].wait_recv()
+        o_fin[other] = fin_r[last][...]
+    total = o_fin[...].reshape(R, LANES)
+    gout_ref[...] = total[:, 0:fields]
+    gbias_ref[...] = total.T[fields : fields + 1, :]
+
+    for copies in (g_copies, c_copies, e_copies):
+        f_copies = f_copies + list(copies.values())
+    for copy in f_copies:
         copy.wait_send()
-    for started in live.values():
-        for copy in started:
-            copy.wait_send()
+    for key in live:
+        if key not in left:
+            gone(*key)
+
+
+def hand_over(gin_ref, gbias_ref, gout_ref, gin_out, gbias_out, gout_out):
+    gin_out[...] = gin_ref[...]
+    gbias_out[...] = gbias_ref[...]
+    gout_out[...] = gout_ref[...]
 
 
 def local(
@@ -347,6 +378,7 @@
     width, fields = output_weight.shape
     R = width // (G * M)
     per = points // M
+    tiles = max(1, per // LANES)
     kind = BF16 if R % 16 == 0 else F32
     chunks = width // S // LANES
     chunk_axes = [ORDERS[n % 4] for n in range(chunks)] + [ORDERS[4]]
@@ -355,31 +387,38 @@
     def dims(axes):
         return tuple(lengths[a] for a in axes)
 
-    r1, s2, r2, a2, s3, r3, a3 = [], [], [], [], [], [], []
+    s1, r1, s2, r2, a2, s3, r3, a3, f32_own, fin = [], [], [], [], [], [], [], [], [], []
     sems = 0
-    for axes in chunk_axes:
+    split = S == 2 and R % 32 == 0
+    for n, axes in enumerate(chunk_axes):
+        rows = R // 2 if split and n == chunks else R
         rest = "yzx".replace(axes[0], "")
         one = rest.replace(axes[1], "")
-        r1.append(pltpu.VMEM((lengths[axes[0]] - 1, *dims(rest), R, LANES), kind))
-        s2.append(pltpu.VMEM((*dims(rest), R, LANES), kind))
-        a2.append(pltpu.VMEM((*dims(rest), R, LANES), F32))
-        r2.append(pltpu.VMEM((lengths[axes[1]] - 1, *dims(one), R, LANES), kind))
-        s3.append(pltpu.VMEM((*dims(one), R, LANES), kind))
-        a3.append(pltpu.VMEM((*dims(one), R, LANES), F32))
-        r3.append(pltpu.VMEM((lengths[axes[2]] - 1, R, LANES), kind))
+        tile = (rows, LANES)
+        s1.append(pltpu.VMEM((*dims("yzx"), *tile), kind))
+        f32_own.append(pltpu.VMEM((*dims("yzx"), *tile), F32))
+        r1.append(pltpu.VMEM((lengths[axes[0]] - 1, *dims(rest), *tile), kind))
+        s2.append(pltpu.VMEM((*dims(rest), *tile), kind))
+        a2.append(pltpu.VMEM((*dims(rest), *tile), F32))
+        r2.append(pltpu.VMEM((lengths[axes[1]] - 1, *dims(one), *tile), kind))
+        s3.append(pltpu.VMEM((*dims(one), *tile), kind))
+        a3.append(pltpu.VMEM((*dims(one), *tile), F32))
+        r3.append(pltpu.VMEM((lengths[axes[2]] - 1, *tile), kind))
+        fin.append(pltpu.VMEM(tile, F32))
         sems += sum(lengths[a] - 1 for a in axes)
-    blocks = (G, MZ, MX, R, LANES)
+    halves = 2 if split else 1
+    o_all = pltpu.VMEM((G, MZ, MX, halves, R // halves, LANES), F32)
+    o_fin = pltpu.VMEM((halves, R // halves, LANES), F32)
     dma = pltpu.SemaphoreType.DMA
     scratch = [
         pltpu.VMEM((points, depth), BF16),
         pltpu.VMEM((depth, points), BF16),
         pltpu.VMEM((depth, width), BF16),
-        pltpu.VMEM((width, fields), BF16),
+        pltpu.VMEM((fields, width), BF16),
         pltpu.VMEM((width, LANES), BF16),
         pltpu.VMEM((LANES, width), BF16),
-        pltpu.VMEM((fields, points), F32),
-        pltpu.VMEM((LANES, points), F32),
-        pltpu.VMEM((points, LANES), F32),
+        pltpu.VMEM((tiles, fields, LANES), F32),
+        pltpu.VMEM((tiles * LANES, LANES), F32),
         pltpu.VMEM((points, width), F32),
         pltpu.VMEM((points, width), BF16),
         pltpu.VMEM((points, width), BF16),
@@ -389,16 +428,10 @@
         pltpu.VMEM((M, per, LANES), BF16),
         pltpu.VMEM((M, per, LANES), BF16),
         pltpu.VMEM((LANES, width), F32),
-        pltpu.VMEM((chunks + 1, *blocks), kind),
-        pltpu.VMEM((chunks + 1, *blocks), kind),
-        pltpu.VMEM((chunks, *blocks), F32),
-        pltpu.VMEM((chunks + 1, *blocks), kind),
-        r1, s2, r2, s3, r3, [a2, a3],
-        pltpu.VMEM((chunks, R, LANES), F32),
-        pltpu.VMEM((chunks, R, LANES), F32),
-        dma((3 + MZ,)), dma((M,)), dma((M,)), dma((M,)), dma((M,)),
+        s1, s1, f32_own, o_all, o_fin, s1, r1, s2, r2, s3, r3, [a2, a3], fin, fin,
+        dma((2 + MZ + tiles,)), dma((M,)), dma((M,)), dma((M,)), dma((M,)),
         dma((chunks + 1,)), dma((chunks + 1,)), dma((sems,)), dma((sems,)),
-        dma((chunks,)), dma((chunks,)),
+        dma((chunks + 1,)), dma((chunks + 1,)),
     ]
     flat, tree = jax.tree.flatten(scratch, is_leaf=lambda leaf: not isinstance(leaf, list))
 
@@ -429,9 +462,21 @@
         ),
         name="crps_gradient",
     )(
-        hidden_states, targets, area_weight[None], var_weight[None], weight_in, bias_in[None],
-        output_weight, output_bias[None],
+        hidden_states, targets.reshape(fields, points // LANES, LANES),
+        area_weight.reshape(points // LANES, LANES), var_weight[None], weight_in, bias_in[None],
+        output_weight.T, output_bias[None],
     )
+    gin, gbias, gout = pl.pallas_call(
+        hand_over,
+        out_shape=(
+            jax.ShapeDtypeStruct((R, width), F32),
+            jax.ShapeDtypeStruct((1, R), F32),
+            jax.ShapeDtypeStruct((R, fields), F32),
+        ),
+        in_specs=[whole, whole, whole],
+        out_specs=(whole, whole, whole),
+        name="results",
+    )(gin, gbias, gout)
     return gin, gbias.reshape(R), gout
 
 

time: 59.5 us -> 49.6 us (0.83)
  local copies, waits for them, and re-layouts: 7.79 us -> 0 us
  Pallas kernels: 50.7 us -> 48.8 us
    unnamed x5 -> x0, local copies, waits for them, and re-layouts: 7.79 us -> none
    pallas_call x1, Pallas kernels: 50.7 us -> 47.1 us  [local(): pl.pallas_call(body, out_shape=(jax.ShapeDtypeStruct((R, width), F32), ja...]
    pallas_call x0 -> x1, Pallas kernels: none -> 1.68 us  [local(): pl.pallas_call(hand_over, out_shape=(jax.ShapeDtypeStruct((R, width), F32...]
where the time goes in v2:
time: 49.6 us; the launch traced here: 49.4 us
  Pallas kernels  48.8 us (98%)
  between operations  0.64 us (1%)
    pallas_call x1, Pallas kernels, local(): pl.pallas_call(body, out_shape=(jax.ShapeDtypeStruct((R, width), F32), ja...  47.1 us
    pallas_call x1, Pallas kernels, local(): pl.pallas_call(hand_over, out_shape=(jax.ShapeDtypeStruct((R, width), F32...  1.68 us

profile of v2, /device:TPU:0, one launch (start us, length us, event | category | flops | bytes accessed | tf_op | source)
XLA Modules:
  0.0 49.4 jit_solution(5737883817072145726)
XLA Ops:
  0.6 47.1 %crps_gradient.1 = (f32[64,1024]{1,0:T(8,128)}, f32[1,64]{1,0:T(1,128)}, f32[64,100]{1,0:T(8,128)}) custom-call(bf16[1,1,1024,1024]{3,2,1,0:T(8,128)(2,1)} %refs_0_.1, f32[100,8,128]{2,1,0:T(8,128)} %bitcast.7, f32[8,128]{1,0:T(8,128)} %bitcast.9, f32[1,100]{1,0:T(1,128)} %bitcast.11, bf16[1024,1024]{1,0:T(8,128)(2,1)} %refs_4_.1, f32[1,1024]{1,0:T(1,128)} %bitcast.10, ...), custom_call_target="tpu_custom_call" | custom-call | flops 5100273664 | bytes 6291456 | tf_op jit(solution)/shard_map/crps_gradient/pallas_call | solution.py:447
  47.8 1.7 %results.1 = (f32[64,1024]{1,0:T(8,128)}, f32[1,64]{1,0:T(1,128)}, f32[64,100]{1,0:T(8,128)}) custom-call(f32[64,1024]{1,0:T(8,128)} %get-tuple-element.9.gin_ref, f32[1,64]{1,0:T(1,128)} %get-tuple-element.10.gbias_ref, f32[64,100]{1,0:T(8,128)} %get-tuple-element.11.gout_ref), custom_call_target="tpu_custom_call" | custom-call | tf_op jit(solution)/shard_map/results/pallas_call | solution.py:469

commit v3 on v2

--- a/solution.py
+++ b/solution.py
@@ -36,12 +36,13 @@
 ):
     G, MZ, MX, S, R = sizes
     M = MZ * MX
-    points, depth = x_v.shape
+    waves, _, pw, depth = x_v.shape
+    points = waves * M * pw
     width = win_v.shape[1]
     fields = wout_v.shape[0]
     tiles = tv.shape[0]
     per = points // M
-    step = points // MZ
+    step = M * pw
     half = width // S
     grid = lax.axis_index("grid")
     me = lax.axis_index("member")
@@ -56,17 +57,13 @@
         copy.start()
         return copy
 
-    def rows_of(i):
-        return pl.multiple_of(lax.rem(mz + 1 + i, MZ) * step, step)
-
+    def fetch_x(w):
+        return fetch(x_hbm.at[:, w], x_v.at[w], 1 + w)
+
+    get_x = [fetch_x(0)]
     get_win = fetch(win_hbm, win_v, 0)
-    get_x = [
-        fetch(x_hbm.at[0, 0, pl.ds(rows_of(i), step)], x_v.at[pl.ds(rows_of(i), step)], 1 + i)
-        for i in range(MZ)
-    ]
-    get_wout = fetch(wout_hbm, wout_v, 1 + MZ)
+    get_wout = fetch(wout_hbm, wout_v, 1 + waves)
     tile = (me * per) // LANES
-    get_t = [fetch(t_hbm.at[:, tile + n], tv.at[n], 2 + MZ + n) for n in range(tiles)]
 
     barrier = pltpu.get_barrier_semaphore()
     for s in range(1, M):
@@ -80,6 +77,8 @@
     w128t[0:fields] = wout_v[...]
     w128[...] = w128t[...].T
     get_win.wait()
+    get_x += [fetch_x(w) for w in range(1, waves)]
+    get_t = [fetch(t_hbm.at[:, tile + n], tv.at[n], 2 + waves + n) for n in range(tiles)]
 
     def remote(src, dst, ss, rs, axis, index):
         return pltpu.make_async_remote_copy(
@@ -87,12 +86,11 @@
             device_id={axis: index}, device_id_type=MESH,
         )
 
-    f_copies = []
-    for i in range(MZ):
-        base = rows_of(i)
-        get_x[i].wait()
-        pre[pl.ds(base, step)] = jnp.dot(
-            x_v[pl.ds(base, step)], win_v[...], preferred_element_type=F32
+    def forward(w):
+        get_x[w].wait()
+        base = w * step
+        pre[base : base + step] = jnp.dot(
+            x_v[w].reshape(step, depth), win_v[...], preferred_element_type=F32
         )
 
         @pl.loop(0, step // 16)
@@ -104,21 +102,24 @@
             hz = 0.5 * z
             act[at] = (hz + hz * t).astype(BF16)
 
-        value = jnp.dot(act[pl.ds(base, step)], w128[...], preferred_element_type=F32)
-        zq = lax.rem(mz + 1 + i, MZ)
-        fsend[pl.ds(zq * MX, MX)] = value.reshape(MX, per, LANES).astype(BF16)
-        if i == 0:
+        value = jnp.dot(act[base : base + step], w128[...], preferred_element_type=F32)
+        fsend[w] = value.reshape(M, pw, LANES).astype(BF16)
+        if w == 0:
             pl.semaphore_wait(barrier, (M - 1) + (G - 1) + 1)
-        for o in range(MX):
-            if i == MZ - 1 and o == 0:
-                continue
-            j = zq * MX + lax.rem(mx + o, MX)
-            copy = remote(
-                fsend.at[j], frecv.at[me], f_ss.at[i * MX + o], f_rs.at[i * MX + o], "member", j
-            )
+        frecv[w, pl.ds(me, 1)] = fsend[w, pl.ds(me, 1)]
+        return spread(w, fsend, frecv, f_ss, f_rs)
+
+    def spread(w, src, dst, ss, rs):
+        copies = []
+        for s in range(1, M):
+            j = lax.rem(me + s, M)
+            sem = w * M + s
+            copy = remote(src.at[w, j], dst.at[w, me], ss.at[sem], rs.at[sem], "member", j)
             copy.start()
-            f_copies.append(copy)
-    frecv[pl.ds(me, 1)] = fsend[pl.ds(me, 1)]
+            copies.append(copy)
+        return copies
+
+    f_copies = [forward(0)]
 
     for n in range(tiles):
         get_t[n].wait()
@@ -133,39 +134,32 @@
     pairwise = (1.0 - eps_fair) / (M * (M - 1))
     loss_scale = M / math.sqrt(S * G * points)
 
-    for copy in f_copies:
-        copy.wait_recv()
-
-    @pl.loop(0, per // 16)
-    def _(n):
-        at = pl.ds(pl.multiple_of(n * 16, 16), 16)
-        seen = tt[pl.ds(pl.multiple_of(shift + n * 16, 16), 16)]
-        scale = (loss_scale * seen[:, fields : fields + 1]) * var
-        target = seen - bout
-        f = [frecv[j, at].astype(F32) for j in range(M)]
-        total = [jnp.zeros((16, LANES), F32) for _ in range(M)]
-        for j in range(M):
-            for k in range(j + 1, M):
-                slope = softened_slope(f[j] - f[k])
-                total[j] = total[j] + slope
-                total[k] = total[k] - slope
-        for j in range(M):
-            g = scale * (softened_slope(f[j] - target) * (1.0 / M) - pairwise * total[j])
-            gsend[j, at] = g.astype(BF16)
-
-    g_copies = {}
-    for i in (1, 2, 0, 3):
-        zq = lax.rem(mz + 1 + i, MZ)
-        for o in range(MX):
-            if i == MZ - 1 and o == 0:
-                continue
-            j = zq * MX + lax.rem(mx + o, MX)
-            copy = remote(
-                gsend.at[j], grecv.at[me], g_ss.at[i * MX + o], g_rs.at[i * MX + o], "member", j
-            )
-            copy.start()
-            g_copies[(i, o)] = copy
-    grecv[pl.ds(me, 1)] = gsend[pl.ds(me, 1)]
+    def pairs(w):
+        for copy in f_copies[w]:
+            copy.wait_recv()
+
+        @pl.loop(0, pw // 16)
+        def _(n):
+            at = pl.ds(pl.multiple_of(n * 16, 16), 16)
+            seen = tt[pl.ds(pl.multiple_of(shift + w * pw + n * 16, 16), 16)]
+            scale = (loss_scale * seen[:, fields : fields + 1]) * var
+            target = seen - bout
+            f = [frecv[w, j, at].astype(F32) for j in range(M)]
+            total = [jnp.zeros((16, LANES), F32) for _ in range(M)]
+            for j in range(M):
+                for k in range(j + 1, M):
+                    slope = softened_slope(f[j] - f[k])
+                    total[j] = total[j] + slope
+                    total[k] = total[k] - slope
+            for j in range(M):
+                g = scale * (softened_slope(f[j] - target) * (1.0 / M) - pairwise * total[j])
+                gsend[w, j, at] = g.astype(BF16)
+
+        grecv[w, pl.ds(me, 1)] = gsend[w, pl.ds(me, 1)]
+        return spread(w, gsend, grecv, g_ss, g_rs)
+
+    f_copies = f_copies + [forward(w) for w in range(1, waves)]
+    g_copies = [pairs(w) for w in range(waves)]
 
     @pl.loop(0, points // 16)
     def _(n):
@@ -176,19 +170,17 @@
         inner = GELU_C + (3.0 * GELU_C * GELU_A) * q
         pre[at] = (0.5 + 0.5 * t) + (0.5 * z) * (1.0 - t * t) * inner
 
-    for n in range(points // 256):
-        xt_v[:, n * 256 : (n + 1) * 256] = x_v[n * 256 : (n + 1) * 256, :].T
+    for w in range(waves):
+        xt_v[:, w * step : (w + 1) * step] = x_v[w].reshape(step, depth).T
     bias_acc[...] = jnp.zeros_like(bias_acc)
 
-    for i in (3, 0, 2, 1):
-        for o in range(MX):
-            if (i, o) in g_copies:
-                g_copies[(i, o)].wait_recv()
-        zq = lax.rem(mz + 2 * MZ - 1 - i, MZ)
-        base = pl.multiple_of(zq * step, step)
-        rows = grecv[pl.ds(zq * MX, MX)].reshape(step, LANES)
+    for w in range(waves):
+        for copy in g_copies[w]:
+            copy.wait_recv()
+        base = w * step
+        rows = grecv[w].reshape(step, LANES)
         back = jnp.dot(rows, w128t[...], preferred_element_type=F32)
-        pre[pl.ds(base, step)] = pre[pl.ds(base, step)] * back
+        pre[base : base + step] = pre[base : base + step] * back
 
         @pl.loop(0, step // 16)
         def _(n):
@@ -320,7 +312,6 @@
             copy.wait_send()
         left.add((n, stage))
 
-    give(0)
     if split:
         csend[last][...] = o_all[:, :, :, other].astype(kind)
         own[last][...] = o_all[:, :, :, core]
@@ -328,8 +319,10 @@
         csend[last][...] = o_all[:, :, :, 0].astype(kind)
         own[last][...] = csend[last][...].astype(F32)
     exchange(last)
+    give(0)
+    first(last)
     keep(0)
-    for n in (0, 1, last):
+    for n in (0, 1):
         first(n)
     for n in range(2, chunks, 2):
         give(n)
@@ -352,10 +345,9 @@
     gout_ref[...] = total[:, 0:fields]
     gbias_ref[...] = total.T[fields : fields + 1, :]
 
-    for copies in (g_copies, c_copies, e_copies):
-        f_copies = f_copies + list(copies.values())
-    for copy in f_copies:
-        copy.wait_send()
+    for copies in (*f_copies, *g_copies, c_copies.values(), e_copies.values()):
+        for copy in copies:
+            copy.wait_send()
     for key in live:
         if key not in left:
             gone(*key)
@@ -379,6 +371,8 @@
     R = width // (G * M)
     per = points // M
     tiles = max(1, per // LANES)
+    waves = 4
+    pw = per // waves
     kind = BF16 if R % 16 == 0 else F32
     chunks = width // S // LANES
     chunk_axes = [ORDERS[n % 4] for n in range(chunks)] + [ORDERS[4]]
@@ -411,7 +405,7 @@
     o_fin = pltpu.VMEM((halves, R // halves, LANES), F32)
     dma = pltpu.SemaphoreType.DMA
     scratch = [
-        pltpu.VMEM((points, depth), BF16),
+        pltpu.VMEM((waves, M, pw, depth), BF16),
         pltpu.VMEM((depth, points), BF16),
         pltpu.VMEM((depth, width), BF16),
         pltpu.VMEM((fields, width), BF16),
@@ -423,13 +417,13 @@
         pltpu.VMEM((points, width), BF16),
         pltpu.VMEM((points, width), BF16),
         pltpu.VMEM((8, width), F32),
-        pltpu.VMEM((M, per, LANES), BF16),
-        pltpu.VMEM((M, per, LANES), BF16),
-        pltpu.VMEM((M, per, LANES), BF16),
-        pltpu.VMEM((M, per, LANES), BF16),
+        pltpu.VMEM((waves, M, pw, LANES), BF16),
+        pltpu.VMEM((waves, M, pw, LANES), BF16),
+        pltpu.VMEM((waves, M, pw, LANES), BF16),
+        pltpu.VMEM((waves, M, pw, LANES), BF16),
         pltpu.VMEM((LANES, width), F32),
         s1, s1, f32_own, o_all, o_fin, s1, r1, s2, r2, s3, r3, [a2, a3], fin, fin,
-        dma((2 + MZ + tiles,)), dma((M,)), dma((M,)), dma((M,)), dma((M,)),
+        dma((2 + waves + tiles,)), *[dma((waves * M,))] * 4,
         dma((chunks + 1,)), dma((chunks + 1,)), dma((sems,)), dma((sems,)),
         dma((chunks + 1,)), dma((chunks + 1,)),
     ]
@@ -462,7 +456,7 @@
         ),
         name="crps_gradient",
     )(
-        hidden_states, targets.reshape(fields, points // LANES, LANES),
+        hidden_states.reshape(M, waves, pw, depth), targets.reshape(fields, points // LANES, LANES),
         area_weight.reshape(points // LANES, LANES), var_weight[None], weight_in, bias_in[None],
         output_weight.T, output_bias[None],
     )

time: 49.6 us -> 47.8 us (0.964)
  Pallas kernels: 48.8 us -> 46.8 us
    pallas_call x1, Pallas kernels: 47.1 us -> 45.1 us  [local(): pl.pallas_call(body, out_shape=(jax.ShapeDtypeStruct((R, width), F32), ja...]
where the time goes in v3:
time: 47.8 us; the launch traced here: 47.4 us
  Pallas kernels  46.8 us (98%)
  between operations  0.64 us (1%)
    pallas_call x1, Pallas kernels, local(): pl.pallas_call(body, out_shape=(jax.ShapeDtypeStruct((R, width), F32), ja...  45.1 us
    pallas_call x1, Pallas kernels, local(): pl.pallas_call(hand_over, out_shape=(jax.ShapeDtypeStruct((R, width), F32...  1.68 us

profile of v3, /device:TPU:0, one launch (start us, length us, event | category | flops | bytes accessed | tf_op | source)
XLA Modules:
  0.0 47.4 jit_solution(1934704584645164929)
XLA Ops:
  0.6 45.1 %crps_gradient.1 = (f32[64,1024]{1,0:T(8,128)}, f32[1,64]{1,0:T(1,128)}, f32[64,100]{1,0:T(8,128)}) custom-call(bf16[8,4,32,1024]{3,2,1,0:T(8,128)(2,1)} %bitcast.8, f32[100,8,128]{2,1,0:T(8,128)} %bitcast.9, f32[8,128]{1,0:T(8,128)} %bitcast.11, f32[1,100]{1,0:T(1,128)} %bitcast.13, bf16[1024,1024]{1,0:T(8,128)(2,1)} %refs_4_.1, f32[1,1024]{1,0:T(1,128)} %bitcast.12, ...), custom_call_target="tpu_custom_call" | custom-call | flops 5100273664 | bytes 6291456 | tf_op jit(solution)/shard_map/crps_gradient/pallas_call | solution.py:441
  45.8 1.7 %results.1 = (f32[64,1024]{1,0:T(8,128)}, f32[1,64]{1,0:T(1,128)}, f32[64,100]{1,0:T(8,128)}) custom-call(f32[64,1024]{1,0:T(8,128)} %get-tuple-element.9.gin_ref, f32[1,64]{1,0:T(1,128)} %get-tuple-element.10.gbias_ref, f32[64,100]{1,0:T(8,128)} %get-tuple-element.11.gout_ref), custom_call_target="tpu_custom_call" | custom-call | tf_op jit(solution)/shard_map/results/pallas_call | solution.py:463
